TPU v7x, 32 devices: a whole 2x2x4 slice. The times are simulated.
32 devices in a mesh: groups: 2 (over x), sect: 8 (over z, y), tp: 2 (over core).
Axes of the slice: x: 2, y: 2, z: 4, core: 2. Of those that a mesh axis runs over, the one named last changes fastest.
Arguments:
- queries: bfloat16 [512, 64, 128], P(('groups', 'sect'), 'tp'), parts along dimension 0, may hold values from -23 to 23
- keys: bfloat16 [512, 128, 2, 128], P(('groups', 'sect'), None, 'tp'), parts along dimension 0, may hold values from -4 to 4
- values: bfloat16 [512, 128, 2, 128], P(('groups', 'sect'), None, 'tp'), parts along dimension 0, may hold values from -12 to 12
- kv_lengths: int32 [512], P(('groups', 'sect')), parts along dimension 0, may hold values from 2 to 128, as said below
- out_proj: bfloat16 [8192, 3584], P('tp', 'sect'), may hold values from -0.0625 to 0.0625
- resid: bfloat16 [512, 3584], P(('groups', 'sect')), parts along dimension 0, may hold values from -6 to 6
- norm_gain: bfloat16 [3584], replicated, may hold values from 0.099609375 to 1.8984375
- experts_chosen: int32 [512, 3], P(('groups', 'sect')), parts along dimension 0, may hold values from 0 to 7, all different within a row; in each aligned block of 32 rows (0 to 31, 32 to 63, ...) at most 16 rows name the same one
- route_probs: float32 [512, 3], P(('groups', 'sect')), parts along dimension 0, may hold values from 0.1 to 1
- expert_home: int32 [8], replicated, may hold values from 0 to 7, each once
- gate_up: bfloat16 [2, 3584, 20480], P(None, None, ('sect', 'tp')), may hold values from -0.09375 to 0.09375
- down_proj: bfloat16 [20480, 3584], P(('sect', 'tp')), may hold values from -0.125 to 0.125
Outputs:
- layer_out: bfloat16 [512, 3584], P(('groups', 'sect'), 'tp'), parts along dimension 0
There are 2 independent parts, one for each index of `groups`. A program takes and returns all parts, laid end to end along the dimension named above; an argument that names none is the same for every part. Nothing has to cross between parts.
Inputs may be any that keep to these rules, and one draw needn't show every extreme that they name: `experts_chosen`: each request names 3 different experts; among the 32 requests of one index of sect no expert is named more than 16 times, a bound that some block reaches there. `expert_home`: each band is named once. `kv_lengths`: in every aligned block of 32 requests some request uses all 128 positions.
All inputs are finite; a program needn't handle non-finite values.
Results may differ from a plain program's by a relative error of at most 0.0058.
Values may be sent and summed in bfloat16 or wider, within the bound.
A program may use at most 128 MiB of HBM per device.

v0:
```python
import math

import jax
import jax.numpy as jnp
from jax import lax
from jax.sharding import PartitionSpec as P


def body(
    queries,
    keys,
    values,
    kv_lengths,
    out_proj,
    resid,
    norm_gain,
    experts_chosen,
    route_probs,
    expert_home,
    gate_up,
    down_proj,
):
    row_count, local_heads, head_dim = queries.shape
    context = keys.shape[1]
    local_kv = keys.shape[2]
    feature_width = resid.shape[1]
    tp_count = lax.axis_size("tp")
    share_width = feature_width // tp_count
    tp_index = lax.axis_index("tp")
    grouped = queries.reshape(row_count, local_kv, local_heads // local_kv, head_dim)
    scores = jnp.einsum(
        "rkgd,rckd->rkgc", grouped, keys, preferred_element_type=jnp.float32
    ) / math.sqrt(head_dim)
    visible = (jnp.arange(context, dtype=jnp.int32)[None, :] < kv_lengths[:, None])[
        :, None, None, :
    ]
    scores = jnp.where(visible, scores, -1e30)
    row_peak = jnp.max(scores, axis=-1, keepdims=True)
    exponent = jnp.where(visible, jnp.exp(scores - row_peak), 0.0)
    weights = (exponent / jnp.sum(exponent, axis=-1, keepdims=True)).astype(jnp.bfloat16)
    heads_out = jnp.einsum(
        "rkgc,rckd->rkgd", weights, values, preferred_element_type=jnp.float32
    ).astype(jnp.bfloat16)
    heads_out = heads_out.reshape(row_count, local_heads * head_dim)
    column_part = jnp.dot(
        lax.all_gather(heads_out, "sect", axis=0, tiled=True),
        out_proj,
        preferred_element_type=jnp.float32,
    )
    partial_value = lax.all_to_all(column_part, "sect", split_axis=0, concat_axis=1, tiled=True)
    summed = lax.psum(partial_value, "tp")
    attended = resid.astype(jnp.float32) + summed
    mean_square = jnp.mean(attended * attended, axis=1, keepdims=True)
    normed = (attended * lax.rsqrt(mean_square + 1e-06) * norm_gain.astype(jnp.float32)).astype(
        jnp.bfloat16
    )
    residual_part = lax.dynamic_slice_in_dim(attended, tp_index * share_width, share_width, 1)
    experts = expert_home.shape[0]
    top_count = experts_chosen.shape[1]
    sections = lax.axis_size("sect")
    band_size = sections // experts
    capacity = row_count // 2
    chosen_flat = experts_chosen.reshape(-1)
    matches = (chosen_flat[:, None] == jnp.arange(experts, dtype=jnp.int32)[None, :]).astype(
        jnp.int32
    )
    earlier = jnp.cumsum(matches, axis=0) - matches
    slot_index = jnp.sum(earlier * matches, axis=1)
    home_band = jnp.sum(matches * expert_home[None, :], axis=1)
    position = home_band * capacity + slot_index
    slot_table = jnp.arange(experts * capacity, dtype=jnp.int32)
    selector = (slot_table[:, None] == position[None, :]).astype(jnp.bfloat16)
    repeated = jnp.repeat(normed, top_count, axis=0)
    packed = jnp.dot(selector, repeated, preferred_element_type=jnp.float32).astype(jnp.bfloat16)
    feature_count = packed.shape[1]
    outbound = jnp.broadcast_to(
        packed.reshape(experts, 1, capacity, feature_count),
        (experts, band_size, capacity, feature_count),
    )
    outbound = outbound.reshape(sections, capacity, feature_count)
    arrived = lax.all_to_all(outbound, "sect", split_axis=0, concat_axis=0, tiled=True)
    senders = arrived.shape[0]
    slot_count = arrived.shape[1]
    flat_rows = arrived.reshape(senders * slot_count, feature_width)
    gate_value = jnp.dot(flat_rows, gate_up[0], preferred_element_type=jnp.float32)
    up_value = jnp.dot(flat_rows, gate_up[1], preferred_element_type=jnp.float32)
    activated = (jax.nn.silu(gate_value) * up_value).astype(jnp.bfloat16)
    activated = activated.reshape(senders, slot_count, down_proj.shape[0])
    down_split = down_proj.reshape(down_proj.shape[0], tp_count, share_width)
    partials = jnp.einsum(
        "sch,hfd->sfcd", activated, down_split, preferred_element_type=jnp.float32
    ).astype(jnp.bfloat16)
    returned = lax.all_to_all(
        partials.reshape(sections * tp_count, capacity, share_width),
        ("sect", "tp"),
        split_axis=0,
        concat_axis=0,
        tiled=True,
    )
    returned = returned.reshape(experts, band_size * tp_count, capacity, share_width)
    per_band = jnp.sum(returned.astype(jnp.float32), axis=1).reshape(
        experts * capacity, share_width
    )
    mixing = jnp.where(
        position[:, None] == slot_table[None, :], route_probs.reshape(-1)[:, None], 0.0
    )
    mixing = jnp.sum(mixing.reshape(row_count, top_count, experts * capacity), axis=1)
    expert_sum = jnp.dot(mixing, per_band, precision=lax.Precision.HIGHEST)
    return (residual_part + expert_sum).astype(jnp.bfloat16)


def solution(mesh):
    in_specs = (
        P(("groups", "sect"), "tp", None),
        P(("groups", "sect"), None, "tp", None),
        P(("groups", "sect"), None, "tp", None),
        P(("groups", "sect")),
        P("tp", "sect"),
        P(("groups", "sect"), None),
        P(),
        P(("groups", "sect"), None),
        P(("groups", "sect"), None),
        P(),
        P(None, None, ("sect", "tp")),
        P(("sect", "tp"), None),
    )
    out_specs = P(("groups", "sect"), "tp")
    return jax.shard_map(body, mesh=mesh, in_specs=in_specs, out_specs=out_specs, check_vma=False)
```

profile of v0, /device:TPU:0, one launch (start us, length us, event | category | flops | bytes accessed | tf_op | source)
XLA Modules:
  0.0 184.4 jit_solution(11782842843537753859)
XLA Ops:
  6.6 0.8 iota_compare_fusion.4
  7.4 0.4 copy-done
  7.8 1.6 fusion.18
  9.4 0.4 fusion.28
  9.7 3.1 %convolution_convert_fusion.1 = bf16[32,32,128]{2,1,0:T(8,128)(2,1)S(1)} fusion(bf16[32,128,1,128]{3,1,2,0:T(8,128)(2,1)} %param.14, f32[32,32]{1,0:T(8,128)S(1)} %fusion.28, f32[32,32,128]{2,1,0:T(8,128)S(1)} %fusion.18, pred[32,128]{1,0:T(8,128)(4,1)S(1)} %iota_compare_fusion.4), kind=kOutput, calls=%fused_computation.22 | convolution fusion | flops 34210944 | bytes 1843200 | tf_op jit(solution)/shard_map/rkgc,rckd->rkgd/dot_general | solution.py:41
  12.8 0.8 copy.38
  13.7 52.1 %all-gather.2.cloned.1.call-done = bf16[256,4096]{1,0:T(8,128)(2,1)} async-done(((bf16[32,4096]{1,0:T(8,128)(2,1)}), bf16[256,4096]{1,0:T(8,128)(2,1)}) %all-gather.2.cloned.1.call-update) | async-done | bytes 2097168 | tf_op jit(solution)/shard_map/all_gather | solution.py:46
  65.8 4.7 %fusion.29 = f32[256,448]{1,0:T(8,128)} fusion(bf16[256,4096]{1,0:T(8,128)(2,1)} %all-gather.2.cloned.1.call-done, bf16[4096,448]{0,1:T(8,128)(2,1)} %param.16), kind=kOutput, calls=%fused_computation.45 | convolution fusion | flops 939524096 | bytes 6225920 | tf_op jit(solution)/shard_map/dot_general | solution.py:45
  70.5 3.5 %all-to-all-start = ((f32[8,32,448]{2,1,0:T(8,128)}), f32[8,32,448]{2,1,0:T(8,128)S(1)}, u32[]{:S(2)}, u32[]{:S(2)}) async-start(f32[8,32,448]{2,1,0:T(8,128)} %bitcast.2), calls=%async_computation | async-start | bytes 1048576 | tf_op jit(solution)/shard_map/all_to_all | solution.py:50
  74.1 0.1 copy.24
  74.2 0.1 eq.42
  74.3 13.8 %all-to-all-done = f32[8,32,448]{2,1,0:T(8,128)S(1)} async-done(((f32[8,32,448]{2,1,0:T(8,128)}), f32[8,32,448]{2,1,0:T(8,128)S(1)}, u32[]{:S(2)}, u32[]{:S(2)}) %all-to-all-start) | async-done | bytes 458784 | tf_op jit(solution)/shard_map/all_to_all | solution.py:50
  88.1 0.3 copy.23
  88.4 1.0 all_to_all.23
  89.5 0.1 reduce_window_sum.11
  89.7 0.2 select_reduce_fusion.2
  89.8 17.4 %all-reduce.2.cloned.1.call-done = f32[32,3584]{1,0:T(8,128)} async-done(((f32[32,3584]{1,0:T(8,128)}), f32[32,3584]{1,0:T(8,128)}) %all-reduce.2.cloned.1.call-update) | async-done | bytes 458768 | tf_op jit(solution)/shard_map/psum | solution.py:51
  107.2 1.2 multiply_reduce_fusion
  108.4 0.1 multiply_convert_fusion
  108.5 0.2 broadcast_in_dim.51
  108.8 0.6 reshape.124
  109.4 0.4 convolution_convert_fusion
  109.8 29.3 %all_to_all.29 = bf16[8,16,3584]{2,1,0:T(8,128)(2,1)S(1)} all-to-all(bf16[8,16,3584]{2,1,0:T(8,128)(2,1)S(1)} %bitcast.59), channel_id=1, replica_groups=mesh['groups'=2,'sect'=8,'tp'=2] {'sect'}, dimensions={0} | all-to-all | bytes 1835008 | tf_op jit(solution)/shard_map/all_to_all | solution.py:81
  139.1 5.1 %fusion.5 = f32[128,1280]{1,0:T(8,128)S(1)} fusion(bf16[128,3584]{1,0:T(8,128)(2,1)S(1)} %bitcast.62, bf16[2,3584,1280]{2,1,0:T(8,128)(2,1)} %param.22), kind=kOutput, calls=%fused_computation.6 | convolution fusion | flops 1174405120 | bytes 10747904 | tf_op jit(solution)/shard_map/dot_general | solution.py:85
  144.3 5.1 %fusion.13 = bf16[128,1280]{1,0:T(8,128)(2,1)S(1)} fusion(bf16[128,3584]{1,0:T(8,128)(2,1)S(1)} %bitcast.63, bf16[2,3584,1280]{2,1,0:T(8,128)(2,1)} %param.22, f32[128,1280]{1,0:T(8,128)S(1)} %fusion.5), kind=kOutput, calls=%fused_computation.13 | convolution fusion | flops 1175388160 | bytes 11075584 | tf_op jit(solution)/shard_map/dot_general | solution.py:86
  149.5 2.3 %fusion.9 = bf16[8,16,2,1792]{3,1,2,0:T(8,128)(2,1)} fusion(bf16[8,16,1280,1]{2,1,3,0:T(8,128)(2,1)S(1)} %bitcast.68, bf16[160,2,8,1792]{3,2,1,0:T(8,128)(2,1)S(1)} %bitcast.67), kind=kOutput, calls=%fused_computation.11 | convolution fusion | flops 1174863872 | bytes 10420224 | tf_op jit(solution)/shard_map/sch,hfd->sfcd/dot_general | solution.py:90
  151.8 3.6 %all-to-all-start.2 = ((bf16[16,16,1792]{2,1,0:T(8,128)(2,1)}), bf16[16,16,1792]{2,1,0:T(8,128)(2,1)S(1)}, u32[]{:S(2)}, u32[]{:S(2)}) async-start(bf16[16,16,1792]{2,1,0:T(8,128)(2,1)} %bitcast.13), calls=%async_computation.2 | async-start | bytes 1835008 | tf_op jit(solution)/shard_map/all_to_all | solution.py:93
  155.4 0.1 add.43
  155.6 0.1 select_reduce_fusion
  155.7 20.5 %all-to-all-done.2 = bf16[16,16,1792]{2,1,0:T(8,128)(2,1)S(1)} async-done(((bf16[16,16,1792]{2,1,0:T(8,128)(2,1)}), bf16[16,16,1792]{2,1,0:T(8,128)(2,1)S(1)}, u32[]{:S(2)}, u32[]{:S(2)}) %all-to-all-start.2) | async-done | bytes 917536 | tf_op jit(solution)/shard_map/all_to_all | solution.py:93
  176.2 0.1 convert_reduce_fusion
  176.3 1.2 fusion.16
  (27 shorter events, 0.3 us)
Async XLA Ops:
  6.5 1.2 copy-start
  6.5 67.6 %copy-start.2 = (bf16[3584]{0:T(1024)(128)(2,1)S(1)}, bf16[3584]{0:T(1024)(128)(2,1)}, u32[]{:S(2)}) copy-start(bf16[3584]{0:T(1024)(128)(2,1)} %param.18) | copy-start | bytes 21508
  6.5 67.6 %copy-start.3 = (s32[32,3]{0,1:T(4,128)S(1)}, s32[32,3]{0,1:T(4,128)}, u32[]{:S(2)}) copy-start(s32[32,3]{0,1:T(4,128)} %param.19) | copy-start | bytes 1156
  6.5 83.1 %copy-start.5 = (s32[8]{0:T(128)S(1)}, s32[8]{0:T(128)}, u32[]{:S(2)}) copy-start(s32[8]{0:T(128)} %param.21) | copy-start | bytes 100
  6.5 100.7 %copy-start.1 = (bf16[32,3584]{1,0:T(8,128)(2,1)S(1)}, bf16[32,3584]{1,0:T(8,128)(2,1)}, u32[]{:S(2)}) copy-start(bf16[32,3584]{1,0:T(8,128)(2,1)} %param.17) | copy-start | bytes 688132
  6.5 59.3 %all-gather.2.cloned.1.call-start = ((), (), s32[]{:S(2)}) async-start(), calls=%async_computation.3 | async-start | bytes 2359296 | tf_op jit(solution)/shard_map/all_gather | solution.py:46
  70.5 17.6 %all-to-all-start = ((f32[8,32,448]{2,1,0:T(8,128)}), f32[8,32,448]{2,1,0:T(8,128)S(1)}, u32[]{:S(2)}, u32[]{:S(2)}) async-start(f32[8,32,448]{2,1,0:T(8,128)} %bitcast.2), calls=%async_computation | async-start | bytes 1048576 | tf_op jit(solution)/shard_map/all_to_all | solution.py:50
  74.0 33.2 %all-reduce.2.cloned.1.call-start = ((), (), s32[]{:S(2)}) async-start(), calls=%async_computation.4 | async-start | bytes 917504 | tf_op jit(solution)/shard_map/psum | solution.py:51
  139.1 10.3 %slice-start = ((s8[9175040]{0:T(1024)(128)(4,1)}), s8[4194304]{0:T(1024)(128)(4,1)S(1)}, s32[]{:S(2)}) async-start(s8[9175040]{0:T(1024)(128)(4,1)} %bitcast.65), calls=%async_computation.5 | async-start | bytes 8388608
  139.1 10.3 %slice-start.1 = ((s8[9175040]{0:T(1024)(128)(4,1)}), s8[4194304]{0:T(1024)(128)(4,1)S(1)}, s32[]{:S(2)}) async-start(s8[9175040]{0:T(1024)(128)(4,1)} %bitcast.65), calls=%async_computation.6 | async-start | bytes 8388608
  144.3 5.2 %slice-start.2 = ((s8[9175040]{0:T(1024)(128)(4,1)}), s8[786432]{0:T(1024)(128)(4,1)S(1)}, s32[]{:S(2)}) async-start(s8[9175040]{0:T(1024)(128)(4,1)} %bitcast.65), calls=%async_computation.7 | async-start | bytes 1572864
  149.4 6.1 %copy-start.4 = (f32[32,3]{0,1:T(4,128)S(1)}, f32[32,3]{0,1:T(4,128)}, u32[]{:S(2)}) copy-start(f32[32,3]{0,1:T(4,128)} %param.20) | copy-start | bytes 1156
  151.8 24.4 %all-to-all-start.2 = ((bf16[16,16,1792]{2,1,0:T(8,128)(2,1)}), bf16[16,16,1792]{2,1,0:T(8,128)(2,1)S(1)}, u32[]{:S(2)}, u32[]{:S(2)}) async-start(bf16[16,16,1792]{2,1,0:T(8,128)(2,1)} %bitcast.13), calls=%async_computation.2 | async-start | bytes 1835008 | tf_op jit(solution)/shard_map/all_to_all | solution.py:93
Sparse Core Ops, SparseCore 0:
  13.8 51.9 all-gather.1
  89.5 17.6 all-reduce.1
where the time goes:
time: 185 us; the launch traced here: 184 us
  waiting for transfers between devices  104 us (56%)
  blocking collectives  29.3 us (16%)
  matrix products  23.5 us (13%)
  between operations  13.6 us (7%)
  starting transfers between devices  7.21 us (4%)
  local copies, waits for them, and re-layouts  3.75 us (2%)
  other arithmetic  3.14 us (2%)
    all_gather x1, waiting for transfers between devices, body(): lax.all_gather(heads_out, 'sect', axis=0, tiled=True)  52.1 us
    all_to_all x1, blocking collectives, body(): lax.all_to_all(outbound, 'sect', split_axis=0, concat_axis=0, tiled=True)  29.3 us
    all_to_all x1, waiting for transfers between devices, body(): lax.all_to_all(partials.reshape(sections * tp_count, capacity, share_widt...  20.5 us
    psum x1, waiting for transfers between devices, body(): summed = lax.psum(partial_value, 'tp')  17.4 us
    all_to_all x1, waiting for transfers between devices, body(): lax.all_to_all(column_part, 'sect', split_axis=0, concat_axis=1, tiled=True)  13.8 us
    dot_general x1, matrix products, body(): jnp.dot(flat_rows, gate_up[1], preferred_element_type=jnp.float32)  5.13 us
    dot_general x1, matrix products, body(): jnp.dot(flat_rows, gate_up[0], preferred_element_type=jnp.float32)  5.11 us
    dot_general x1, matrix products, body(): jnp.dot(lax.all_gather(heads_out, 'sect', axis=0, tiled=True), out_proj,...  4.74 us
  transfers between devices with their start and end apart: 4, of which 4 were waited for; matrix products, arithmetic and copies ran while one was open for 0% of the time, Pallas kernels for 0%

commit v1 on v0

v1 whole, which is shorter than its diff:
```python
import functools
import math

import jax
import jax.numpy as jnp
from jax import lax
from jax.experimental import pallas as pl
from jax.experimental.pallas import tpu as pltpu
from jax.sharding import PartitionSpec as P

CAP_SHARE = 2


def each(count, start, f):
    if count <= 8:
        for i in range(start, count):
            f(i)
    else:

        def step(i, carry):
            f(i)
            return carry

        lax.fori_loop(start, count, step, 0)


def layer_kernel(
    S,
    NC,
    NR,
    heads,
    wo_hbm,
    resid,
    gain,
    selector,
    mixing,
    wg_hbm,
    wd_hbm,
    att_out,
    es_out,
    wo,
    wg,
    wd,
    gath,
    part,
    tp_in,
    feat_out,
    feat_in,
    normed,
    attended,
    packed,
    xbuf,
    acc,
    act,
    down_out,
    down_in,
    ret_out,
    ret_in,
    w_sem,
    ring_send,
    ring_recv,
    tpx_send,
    tpx_recv,
    feat_send,
    feat_recv,
    nx_send,
    nx_recv,
    disp_send,
    disp_recv,
    share_send,
    share_recv,
    dx_send,
    dx_recv,
    ret_send,
    ret_recv,
):
    f32, bf16 = jnp.float32, jnp.bfloat16
    s = lax.axis_index("sect")
    t = lax.axis_index("tp")
    rows, heads_width = heads.shape
    half = rows // 2
    F = wo.shape[1]
    D = F * S
    cap = xbuf.shape[1] // S
    HB = S // 2
    CB = HB // NC
    W = ret_in.shape[2]
    ring_half = S // 2

    def ring_index(q):
        return jnp.where(q < ring_half, 2 * q, 2 * (S - 1 - q) + 1)

    pos = jnp.where(s % 2 == 0, s // 2, S - 1 - (s - 1) // 2)

    def owner(rel):
        return ring_index((pos + rel + S) % S)

    right, left = owner(1), owner(-1)

    def remote(src, dst, ss, rs, **dev):
        return pltpu.make_async_remote_copy(
            src_ref=src,
            dst_ref=dst,
            send_sem=ss,
            recv_sem=rs,
            device_id=dev,
            device_id_type=pl.DeviceIdType.MESH,
        )

    copies = [
        pltpu.make_async_copy(wo_hbm, wo, w_sem.at[0]),
        pltpu.make_async_copy(wg_hbm.at[0], wg.at[0], w_sem.at[1]),
        pltpu.make_async_copy(wg_hbm.at[1], wg.at[1], w_sem.at[2]),
        pltpu.make_async_copy(wd_hbm, wd, w_sem.at[3]),
    ]
    for c in copies:
        c.start()

    barrier = pltpu.get_barrier_semaphore()
    pl.semaphore_signal(
        barrier, inc=1, device_id={"tp": 1 - t}, device_id_type=pl.DeviceIdType.MESH
    )

    def greet(d):
        pl.semaphore_signal(
            barrier,
            inc=1,
            device_id={"sect": (s + d) % S},
            device_id_type=pl.DeviceIdType.MESH,
        )

    each(S, 1, greet)
    pl.semaphore_wait(barrier, S)

    def slot(k, direction):
        if k == 0:
            return 0
        return 2 * k - 1 if direction == 0 or k == ring_half else 2 * k

    def ring_copy(k, direction, h):
        src_row = slot(k - 1, direction) * rows + h * half
        dst_row = slot(k, direction) * rows + h * half
        src = heads.at[pl.ds(h * half, half)] if k == 1 else gath.at[pl.ds(src_row, half)]
        return remote(
            src,
            gath.at[pl.ds(dst_row, half)],
            ring_send.at[direction, k - 1, h],
            ring_recv.at[direction, k - 1, h],
            sect=right if direction == 0 else left,
        )

    def ring_pairs(k):
        return [(0, 0), (1, 1)] if k == ring_half else [(0, 0), (1, 0), (0, 1), (1, 1)]

    for direction, h in [(0, 0), (1, 1), (0, 1), (1, 0)]:
        ring_copy(1, direction, h).start()

    def exchange(o):
        return remote(
            part.at[o, 1 - t],
            tp_in.at[o],
            tpx_send.at[o],
            tpx_recv.at[o],
            tp=1 - t,
        )

    def rel_of(o):
        if o == 0:
            return 0
        k = (o + 1) // 2
        return -k if o % 2 == 1 else k

    def feature_copy(o):
        return remote(
            feat_out.at[o],
            feat_in.at[s],
            feat_send.at[o],
            feat_recv.at[s],
            sect=owner(rel_of(o)),
        )

    def feature_arrival(j):
        return remote(feat_out.at[0], feat_in.at[j], feat_send.at[0], feat_recv.at[j], sect=j)

    def finish(o):
        exchange(o).wait_recv()
        total = part[o, t] + tp_in[o]
        if o == 0:
            feat_in[s] = total.astype(bf16)
        else:
            feat_out[o] = total.astype(bf16)
            feature_copy(o).start()

    def project(block, first, count):
        product = jnp.dot(block, wo[...], preferred_element_type=f32)
        for b in range(count):
            for h in range(2):
                part[first + b, h] = product[b * rows + h * half : b * rows + (h + 1) * half]
            exchange(first + b).start()

    copies[0].wait()
    project(heads[...], 0, 1)
    waiting = [0]
    for k in range(1, ring_half + 1):
        for direction, h in ring_pairs(k):
            ring_copy(k, direction, h).wait_recv()
            if k < ring_half and (direction, h) in ring_pairs(k + 1):
                ring_copy(k + 1, direction, h).start()
        if k < ring_half:
            project(gath[pl.ds((2 * k - 1) * rows, 2 * rows)], 2 * k - 1, 2)
            for o in waiting:
                finish(o)
            waiting = [2 * k - 1, 2 * k]
        else:
            project(gath[pl.ds((S - 1) * rows, rows)], S - 1, 1)
            for o in waiting:
                finish(o)
            finish(S - 1)

    def await_features(d):
        feature_arrival((s + d) % S).wait_recv()

    each(S, 1, await_features)
    squares = jnp.zeros((half, 1), f32)
    for j in range(S):
        a = resid[t, j].astype(f32) + feat_in[j].astype(f32)
        attended[t, j] = a
        squares = squares + jnp.sum(a * a, axis=1, keepdims=True)
    scale = lax.rsqrt(squares * (1.0 / D) + 1e-06)
    for j in range(S):
        normed[t, j] = (attended[t, j] * scale * gain[j].astype(f32)).astype(bf16)
    normed_copy = remote(normed.at[t], normed.at[t], nx_send.at[0], nx_recv.at[0], tp=1 - t)
    normed_copy.start()
    theirs = pl.ds((1 - t) * HB, HB)
    att_copy = remote(
        attended.at[t, theirs], attended.at[t, theirs], nx_send.at[1], nx_recv.at[1], tp=1 - t
    )
    att_copy.start()
    normed_arrival = remote(
        normed.at[1 - t], normed.at[1 - t], nx_send.at[0], nx_recv.at[0], tp=1 - t
    )
    normed_arrival.wait_recv()

    mine = pl.ds(s * cap, cap)

    def dispatch_copy(c, d):
        dest = (s + d) % S
        return remote(
            packed.at[pl.ds(c * CB, CB), pl.ds(dest * cap, cap)],
            xbuf.at[pl.ds(t * HB + c * CB, CB), mine],
            disp_send.at[c, d],
            disp_recv.at[c, d],
            sect=dest,
        )

    def dispatch_arrival(c, d):
        sender = (s - d + S) % S
        return remote(
            packed.at[pl.ds(c * CB, CB), pl.ds(sender * cap, cap)],
            xbuf.at[pl.ds(t * HB + c * CB, CB), pl.ds(sender * cap, cap)],
            disp_send.at[c, d],
            disp_recv.at[c, d],
            sect=sender,
        )

    def share_copy(c, core):
        blocks = xbuf.at[pl.ds(core * HB + c * CB, CB)]
        return remote(blocks, blocks, share_send.at[c], share_recv.at[c], tp=1 - t)

    sel = selector[...]
    for c in range(NC):
        for b in range(CB):
            i = c * CB + b
            j = t * HB + i
            block = jnp.concatenate([normed[0, j], normed[1, j]], axis=0)
            packed[i] = jnp.dot(sel, block, preferred_element_type=f32).astype(bf16)
            xbuf[j, mine] = packed[i, mine]
        each(S, 1, lambda d: dispatch_copy(c, d).start())

    copies[1].wait()
    copies[2].wait()

    def accumulate(c, core):
        for b in range(CB):
            j = core * HB + c * CB + b
            x = xbuf[j]
            k_rows = pl.ds(pl.multiple_of(j * F, 16), F)
            for m in range(2):
                acc[m] += jnp.dot(x, wg[m, k_rows, :], preferred_element_type=f32)

    acc[...] = jnp.zeros_like(acc)
    for c in range(NC):
        each(S, 1, lambda d: dispatch_arrival(c, d).wait_recv())
        share_copy(c, t).start()
        accumulate(c, t)
        if c > 0:
            share_copy(c - 1, 1 - t).wait_recv()
            accumulate(c - 1, 1 - t)
    share_copy(NC - 1, 1 - t).wait_recv()
    accumulate(NC - 1, 1 - t)

    gate_value = acc[0]
    act[...] = (gate_value / (1.0 + jnp.exp(-gate_value)) * acc[1]).astype(bf16)
    copies[3].wait()

    def down_columns(core, r):
        return pl.ds(pl.multiple_of(core * (NR * W) + r * W, 128), W)

    def down_copy(r):
        return remote(down_out.at[r], down_in.at[r], dx_send.at[r], dx_recv.at[r], tp=1 - t)

    def return_copy(r, d):
        dest = (s + d) % S
        return remote(
            ret_out.at[r, pl.ds(dest * cap, cap)],
            ret_in.at[r, mine],
            ret_send.at[r, d],
            ret_recv.at[r, d],
            sect=dest,
        )

    def return_arrival(r, d):
        rows_of = pl.ds(((s - d + S) % S) * cap, cap)
        return remote(
            ret_out.at[r, rows_of],
            ret_in.at[r, rows_of],
            ret_send.at[r, d],
            ret_recv.at[r, d],
            sect=(s - d + S) % S,
        )

    for r in range(NR):
        down_out[r] = jnp.dot(
            act[...], wd[:, down_columns(1 - t, r)], preferred_element_type=f32
        ).astype(bf16)
        down_copy(r).start()
        own = jnp.dot(
            act[...], wd[:, down_columns(t, r)], preferred_element_type=f32
        ).astype(bf16)
        down_copy(r).wait_recv()
        ret_out[r] = (own.astype(f32) + down_in[r].astype(f32)).astype(bf16)
        each(S, 1, lambda d: return_copy(r, d).start())
        ret_in[r, mine] = ret_out[r, mine]

    mix = mixing[...]
    mix_high = mix.astype(bf16)
    rest = mix - mix_high.astype(f32)
    mix_mid = rest.astype(bf16)
    mix_low = (rest - mix_mid.astype(f32)).astype(bf16)

    att_arrival = remote(
        attended.at[1 - t, pl.ds(t * HB, HB)],
        attended.at[1 - t, pl.ds(t * HB, HB)],
        nx_send.at[1],
        nx_recv.at[1],
        tp=1 - t,
    )
    att_arrival.wait_recv()
    for h in range(2):
        att_out[h] = attended[h, pl.ds(t * HB, HB)]
    for r in range(NR):
        each(S, 1, lambda d: return_arrival(r, d).wait_recv())
        got = ret_in[r]
        es_out[:, r * W : (r + 1) * W] = (
            jnp.dot(mix_high, got, preferred_element_type=f32)
            + jnp.dot(mix_mid, got, preferred_element_type=f32)
            + jnp.dot(mix_low, got, preferred_element_type=f32)
        )

    for k in range(1, ring_half + 1):
        for direction, h in ring_pairs(k):
            ring_copy(k, direction, h).wait_send()
    for o in range(S):
        exchange(o).wait_send()
        if o > 0:
            feature_copy(o).wait_send()
    normed_copy.wait_send()
    att_copy.wait_send()
    for c in range(NC):
        each(S, 1, lambda d: dispatch_copy(c, d).wait_send())
        share_copy(c, t).wait_send()
    for r in range(NR):
        down_copy(r).wait_send()
        each(S, 1, lambda d: return_copy(r, d).wait_send())


def layer_call(S, heads, out_proj, resid, gain, selector, mixing, gate_up, down_proj):
    f32, bf16 = jnp.float32, jnp.bfloat16
    rows, heads_width = heads.shape
    half = rows // 2
    F = out_proj.shape[1]
    D = F * S
    hidden = down_proj.shape[0]
    slots = selector.shape[0]
    HB = S // 2
    NC = math.gcd(HB, 4)
    NR = 2
    W = D // 2 // NR
    dma = pltpu.SemaphoreType.DMA
    vmem = pl.BlockSpec(memory_space=pltpu.VMEM)
    hbm = pl.BlockSpec(memory_space=pl.ANY)
    return pl.pallas_call(
        functools.partial(layer_kernel, S, NC, NR),
        out_shape=(
            jax.ShapeDtypeStruct((2, HB, half, F), f32),
            jax.ShapeDtypeStruct((rows, D // 2), f32),
        ),
        in_specs=[vmem, hbm, vmem, vmem, vmem, vmem, hbm, hbm],
        out_specs=(vmem, vmem),
        scratch_shapes=[
            pltpu.VMEM(out_proj.shape, bf16),
            pltpu.VMEM(gate_up.shape, bf16),
            pltpu.VMEM(down_proj.shape, bf16),
            pltpu.VMEM((S * rows, heads_width), bf16),
            pltpu.VMEM((S, 2, half, F), f32),
            pltpu.VMEM((S, half, F), f32),
            pltpu.VMEM((S, half, F), bf16),
            pltpu.VMEM((S, half, F), bf16),
            pltpu.VMEM((2, S, half, F), bf16),
            pltpu.VMEM((2, S, half, F), f32),
            pltpu.VMEM((HB, slots, F), bf16),
            pltpu.VMEM((S, slots, F), bf16),
            pltpu.VMEM((2, slots, hidden), f32),
            pltpu.VMEM((slots, hidden), bf16),
            pltpu.VMEM((NR, slots, W), bf16),
            pltpu.VMEM((NR, slots, W), bf16),
            pltpu.VMEM((NR, slots, W), bf16),
            pltpu.VMEM((NR, slots, W), bf16),
            dma((4,)),
            dma((2, S // 2, 2)),
            dma((2, S // 2, 2)),
            dma((S,)),
            dma((S,)),
            dma((S,)),
            dma((S,)),
            dma((2,)),
            dma((2,)),
            dma((NC, S)),
            dma((NC, S)),
            dma((NC,)),
            dma((NC,)),
            dma((NR,)),
            dma((NR,)),
            dma((NR, S)),
            dma((NR, S)),
        ],
        compiler_params=pltpu.CompilerParams(
            collective_id=0, has_side_effects=True, vmem_limit_bytes=56 * 1024 * 1024
        ),
        cost_estimate=pl.CostEstimate(
            flops=2 * S * rows * heads_width * F + 6 * slots * D * hidden,
            bytes_accessed=2 * (out_proj.size + gate_up.size + down_proj.size),
            transcendentals=slots * hidden,
        ),
    )(heads, out_proj, resid, gain, selector, mixing, gate_up, down_proj)


def body(
    queries,
    keys,
    values,
    kv_lengths,
    out_proj,
    resid,
    norm_gain,
    experts_chosen,
    route_probs,
    expert_home,
    gate_up,
    down_proj,
):
    row_count, local_heads, head_dim = queries.shape
    context = keys.shape[1]
    local_kv = keys.shape[2]
    width = resid.shape[1]
    experts = expert_home.shape[0]
    top_count = experts_chosen.shape[1]
    S = lax.axis_size("sect")
    half = row_count // 2
    F = width // S
    band_size = S // experts
    capacity = row_count // CAP_SHARE

    grouped = queries.reshape(row_count, local_kv, local_heads // local_kv, head_dim)
    scores = jnp.einsum(
        "rkgd,rckd->rkgc", grouped, keys, preferred_element_type=jnp.float32
    ) / math.sqrt(head_dim)
    visible = (jnp.arange(context, dtype=jnp.int32)[None, :] < kv_lengths[:, None])[
        :, None, None, :
    ]
    scores = jnp.where(visible, scores, -1e30)
    row_peak = jnp.max(scores, axis=-1, keepdims=True)
    exponent = jnp.where(visible, jnp.exp(scores - row_peak), 0.0)
    weights = (exponent / jnp.sum(exponent, axis=-1, keepdims=True)).astype(jnp.bfloat16)
    heads_out = jnp.einsum(
        "rkgc,rckd->rkgd", weights, values, preferred_element_type=jnp.float32
    ).astype(jnp.bfloat16)
    heads_out = heads_out.reshape(row_count, local_heads * head_dim)

    chosen_flat = experts_chosen.reshape(-1)
    matches = (chosen_flat[:, None] == jnp.arange(experts, dtype=jnp.int32)[None, :]).astype(
        jnp.int32
    )
    earlier = jnp.cumsum(matches, axis=0) - matches
    slot_index = jnp.sum(earlier * matches, axis=1)
    home_band = jnp.sum(matches * expert_home[None, :], axis=1)
    position = (home_band * capacity + slot_index).reshape(row_count, top_count)
    table = jnp.arange(S * capacity, dtype=jnp.int32)
    table = (table // capacity) // band_size * capacity + table % capacity
    hits = position[:, :, None] == table[None, None, :]
    selector = jnp.any(hits, axis=1).T.astype(jnp.bfloat16)
    mixing = jnp.sum(jnp.where(hits, route_probs[:, :, None], 0.0), axis=1)

    resid_blocks = resid.reshape(2, half, S, F).transpose(0, 2, 1, 3)
    gain_blocks = norm_gain.reshape(S, 1, F)
    att, expert_sum = layer_call(
        S, heads_out, out_proj, resid_blocks, gain_blocks, selector, mixing, gate_up, down_proj
    )
    att = att.transpose(0, 2, 1, 3).reshape(row_count, width // 2)
    return (att + expert_sum).astype(jnp.bfloat16)


def solution(mesh):
    in_specs = (
        P(("groups", "sect"), "tp", None),
        P(("groups", "sect"), None, "tp", None),
        P(("groups", "sect"), None, "tp", None),
        P(("groups", "sect")),
        P("tp", "sect"),
        P(("groups", "sect"), None),
        P(),
        P(("groups", "sect"), None),
        P(("groups", "sect"), None),
        P(),
        P(None, None, ("sect", "tp")),
        P(("sect", "tp"), None),
    )
    out_specs = P(("groups", "sect"), "tp")
    return jax.shard_map(body, mesh=mesh, in_specs=in_specs, out_specs=out_specs, check_vma=False)
```

time: 185 us -> 92.3 us (0.50)
  waiting for transfers between devices: 104 us -> 0 us
  Pallas kernels: 0 us -> 68 us
  blocking collectives: 29.3 us -> 0 us
  matrix products: 23.5 us -> 4.65 us
  between operations: 13.6 us -> 0.07 us
  local copies, waits for them, and re-layouts: 3.75 us -> 13.8 us
  starting transfers between devices: 7.21 us -> 0 us
  other arithmetic: 3.14 us -> 5.33 us
    pallas_call x0 -> x1, Pallas kernels: none -> 68 us  [layer_call(): pl.pallas_call(functools.partial(layer_kernel, S, NC, NR), out_shape=(jax...]
    all_gather x1 -> x0, waiting for transfers between devices: 52.1 us -> none  [body(): lax.all_gather(heads_out, 'sect', axis=0, tiled=True)]
    all_to_all x2 -> x0, waiting for transfers between devices: 34.3 us -> none  [the longest x1 20.5 us: body(): lax.all_to_all(partials.reshape(sections * tp_count, capacity, share_widt...]
    all_to_all x1 -> x0, blocking collectives: 29.3 us -> none  [body(): lax.all_to_all(outbound, 'sect', split_axis=0, concat_axis=0, tiled=True)]
    dot_general x6 -> x0, matrix products: 18.9 us -> none  [the longest x1 5.13 us: body(): jnp.dot(flat_rows, gate_up[1], preferred_element_type=jnp.float32)]
    psum x1 -> x0, waiting for transfers between devices: 17.4 us -> none  [body(): summed = lax.psum(partial_value, 'tp')]
    all_to_all x2 -> x0, starting transfers between devices: 7.12 us -> none  [the longest x1 3.63 us: body(): lax.all_to_all(partials.reshape(sections * tp_count, capacity, share_widt...]
    unnamed x20 -> x5, local copies, waits for them, and re-layouts: 1.33 us -> 7.97 us
  transfers between devices with their start and end apart: 4 -> 0, of which waited for: 4 -> 0; matrix products, arithmetic and copies ran while one was open for 0% -> 0% of each run, Pallas kernels for 0% -> 0%
where the time goes in v1:
time: 92.3 us; the launch traced here: 91.8 us
  Pallas kernels  68 us (74%)
  local copies, waits for them, and re-layouts  13.8 us (15%)
  other arithmetic  5.33 us (6%)
  matrix products  4.65 us (5%)
    pallas_call x1, Pallas kernels, layer_call(): pl.pallas_call(functools.partial(layer_kernel, S, NC, NR), out_shape=(jax...  68 us
    unnamed x5, local copies, waits for them, and re-layouts  7.97 us
    dot_general x1, matrix products, body(): jnp.einsum('rkgc,rckd->rkgd', weights, values, preferred_element_type=jnp...  3.05 us
    reshape x2, local copies, waits for them, and re-layouts, body(): resid_blocks = resid.reshape(2, half, S, F).transpose(0, 2, 1, 3)  2.05 us

profile of v1, /device:TPU:0, one launch (start us, length us, event | category | flops | bytes accessed | tf_op | source)
XLA Modules:
  0.0 91.8 jit_solution(1559450857160287903)
XLA Ops:
  0.0 0.0 copy-start
  0.0 0.8 iota_compare_fusion.1
  0.8 1.4 %reshape.107.gain = bf16[8,1,448]{2,1,0:T(2,128)(2,1)} reshape(bf16[3584]{0:T(1024)(128)(2,1)} %param.18) | data formatting | bytes 14336 | tf_op jit(solution)/shard_map/reshape | solution.py:515
  2.2 0.8 copy.31
  3.0 0.1 eq.30
  3.1 0.1 fusion.9
  3.2 0.1 reduce_window_sum.11
  3.3 0.8 select_reduce_fusion.1
  4.2 0.1 add.38
  4.3 0.1 copy.32
  4.3 0.1 compare_reduce_fusion
  4.5 1.4 %fusion.8.mixing = f32[32,128]{1,0:T(8,128)} fusion(f32[32,3]{0,1:T(4,128)} %param.20, s32[128]{0:T(128)S(1)} %fusion.10, s32[32,3]{0,1:T(4,128)S(1)} %copy.32), kind=kLoop, calls=%fused_computation.16 | loop fusion | flops 32768 | bytes 17664 | tf_op jit(solution)/shard_map/reduce_sum | solution.py:512
  5.8 0.7 copy.33
  6.6 1.3 %reshape.104 = bf16[2,16,8,448]{3,2,1,0:T(8,128)(2,1)S(1)} reshape(bf16[32,3584]{1,0:T(8,128)(2,1)} %param.17) | data formatting | bytes 458752 | tf_op jit(solution)/shard_map/reshape | solution.py:514
  7.8 0.8 copy.41
  8.6 0.0 copy-done
  8.6 1.6 %fusion.2 = f32[32,32,128]{2,1,0:T(8,128)S(1)} fusion(bf16[32,32,128]{2,1,0:T(8,128)(2,1)} %param.12, bf16[32,128,1,128]{3,1,2,0:T(8,128)(2,1)S(1)} %copy-done, pred[32,128]{1,0:T(8,128)(4,1)S(1)} %iota_compare_fusion.1), kind=kOutput, calls=%fused_computation.3 | convolution fusion | flops 33816576 | bytes 1839104 | tf_op jit(solution)/shard_map/rkgd,rckd->rkgc/dot_general | solution.py:485
  10.2 0.4 fusion.14
  10.6 3.1 %convolution_convert_fusion = bf16[32,32,128]{2,1,0:T(8,128)(2,1)S(1)} fusion(bf16[32,128,1,128]{3,1,2,0:T(8,128)(2,1)} %param.14, f32[32,32]{1,0:T(8,128)S(1)} %fusion.14, f32[32,32,128]{2,1,0:T(8,128)S(1)} %fusion.2, pred[32,128]{1,0:T(8,128)(4,1)S(1)} %iota_compare_fusion.1), kind=kOutput, calls=%fused_computation.6 | convolution fusion | flops 34210944 | bytes 1843200 | tf_op jit(solution)/shard_map/rkgc,rckd->rkgd/dot_general | solution.py:495
  13.6 0.8 copy.40
  14.4 6.4 %copy.34.wo_hbm = bf16[4096,448]{1,0:T(8,128)(2,1)} copy(bf16[4096,448]{0,1:T(8,128)(2,1)} %param.16) | data formatting | bytes 7340032 | tf_op args[4]
  20.8 68.0 %shard_map.118 = (f32[2,4,16,448]{3,2,1,0:T(8,128)}, f32[32,1792]{1,0:T(8,128)}) custom-call(bf16[32,4096]{1,0:T(8,128)(2,1)} %bitcast.19, bf16[4096,448]{1,0:T(8,128)(2,1)} %copy.34.wo_hbm, bf16[2,8,16,448]{3,2,1,0:T(8,128)(2,1)} %bitcast.18, bf16[8,1,448]{2,1,0:T(2,128)(2,1)} %reshape.107.gain, bf16[128,32]{1,0:T(8,128)(2,1)} %bitcast.22, ...), custom_call_target="tpu_custom_call" | custom-call | flops 4462739456 | bytes 31195136 | tf_op jit(solution)/shard_map/pallas_call | solution.py:402
  88.8 1.1 %copy.36 = f32[2,16,4,448]{3,2,1,0:T(4,128)S(1)} copy(f32[2,16,4,448]{3,1,2,0:T(8,128)} %bitcast.20) | data formatting | bytes 458752 | tf_op jit(solution)/shard_map/transpose | solution.py:519
  90.0 0.3 reshape.106
  90.2 1.6 %add_convert_fusion = bf16[32,1792]{1,0:T(8,128)(2,1)} fusion(f32[32,1792]{1,0:T(8,128)S(1)} %reshape.106, f32[32,1792]{1,0:T(8,128)} %get-tuple-element.8), kind=kLoop, calls=%fused_computation.13 | loop fusion | flops 114688 | bytes 573440 | tf_op jit(solution)/shard_map/convert_element_type | solution.py:520
  (3 shorter events, 0.0 us)
Async XLA Ops:
  0.0 8.6 %copy-start = (bf16[32,128,1,128]{3,1,2,0:T(8,128)(2,1)S(1)}, bf16[32,128,1,128]{3,1,2,0:T(8,128)(2,1)}, u32[]{:S(2)}) copy-start(bf16[32,128,1,128]{3,1,2,0:T(8,128)(2,1)} %param.13) | copy-start | bytes 3145732

commit v2 on v1

v2 whole, which is shorter than its diff:
```python
import functools
import math

import jax
import jax.numpy as jnp
from jax import lax
from jax.experimental import pallas as pl
from jax.experimental.pallas import tpu as pltpu
from jax.sharding import PartitionSpec as P

CAP_SHARE = 2


def each(count, start, f):
    if count <= 8:
        for i in range(start, count):
            f(i)
    else:

        def step(i, carry):
            f(i)
            return carry

        lax.fori_loop(start, count, step, 0)


def layer_kernel(
    S,
    widths,
    lengths,
    home,
    q_hbm,
    k_hbm,
    v_hbm,
    wo_hbm,
    resid,
    gain,
    chosen,
    probs,
    wg_hbm,
    wd_hbm,
    out,
    q,
    kc,
    vc,
    wo,
    wg,
    wd,
    attn,
    gath,
    part,
    tp_in,
    feat_out,
    feat_in,
    normed,
    attended,
    selector,
    mixing,
    packed,
    xbuf,
    acc,
    act,
    down_out,
    down_in,
    ret_out,
    ret_in,
    kv_sem,
    w_sem,
    ring_send,
    ring_recv,
    tpx_send,
    tpx_recv,
    feat_send,
    feat_recv,
    nx_send,
    nx_recv,
    disp_send,
    disp_recv,
    share_send,
    share_recv,
    dx_send,
    dx_recv,
    ret_send,
    ret_recv,
):
    f32, bf16 = jnp.float32, jnp.bfloat16
    s = lax.axis_index("sect")
    t = lax.axis_index("tp")
    rows, heads_count, head_dim = q.shape
    context = kc.shape[1]
    half = rows // 2
    F = wo.shape[0]
    D = F * S
    H = D // 2
    cap = xbuf.shape[0] // S
    experts = home.shape[0]
    band_size = S // experts
    top_count = chosen.shape[0]
    NC = len(widths)
    starts = [sum(widths[:c]) for c in range(NC)]
    ring_half = S // 2

    def ring_index(p):
        return jnp.where(p < ring_half, 2 * p, 2 * (S - 1 - p) + 1)

    pos = jnp.where(s % 2 == 0, s // 2, S - 1 - (s - 1) // 2)

    def owner(rel):
        return ring_index((pos + rel + S) % S)

    right, left = owner(1), owner(-1)

    def remote(src, dst, ss, rs, **dev):
        return pltpu.make_async_remote_copy(
            src_ref=src,
            dst_ref=dst,
            send_sem=ss,
            recv_sem=rs,
            device_id=dev,
            device_id_type=pl.DeviceIdType.MESH,
        )

    kv_copies = []
    for h in range(2):
        block = pl.ds(h * half, half)
        kv_copies.append(
            [
                pltpu.make_async_copy(a.at[block], b.at[block], kv_sem.at[i, h])
                for i, (a, b) in enumerate([(q_hbm, q), (k_hbm, kc), (v_hbm, vc)])
            ]
        )
        for c in kv_copies[h]:
            c.start()
    copies = [
        pltpu.make_async_copy(wo_hbm, wo, w_sem.at[0]),
        pltpu.make_async_copy(wg_hbm.at[0], wg.at[0], w_sem.at[1]),
        pltpu.make_async_copy(wg_hbm.at[1], wg.at[1], w_sem.at[2]),
        pltpu.make_async_copy(wd_hbm, wd, w_sem.at[3]),
    ]
    copies[0].start()

    barrier = pltpu.get_barrier_semaphore()
    pl.semaphore_signal(
        barrier, inc=1, device_id={"tp": 1 - t}, device_id_type=pl.DeviceIdType.MESH
    )

    def greet(d):
        pl.semaphore_signal(
            barrier,
            inc=1,
            device_id={"sect": (s + d) % S},
            device_id_type=pl.DeviceIdType.MESH,
        )

    each(S, 1, greet)

    def slot(k, direction):
        if k == 0:
            return 0
        return 2 * k - 1 if direction == 0 or k == ring_half else 2 * k

    def ring_copy(k, direction, h):
        return remote(
            gath.at[pl.ds(slot(k - 1, direction) * rows + h * half, half)],
            gath.at[pl.ds(slot(k, direction) * rows + h * half, half)],
            ring_send.at[direction, k - 1, h],
            ring_recv.at[direction, k - 1, h],
            sect=right if direction == 0 else left,
        )

    def ring_pairs(k):
        return [(0, 0), (1, 1)] if k == ring_half else [(0, 0), (1, 0), (0, 1), (1, 1)]

    positions = lax.broadcasted_iota(jnp.int32, (heads_count, context), 1)
    inverse_root = 1.0 / math.sqrt(head_dim)
    for h in range(2):
        for c in kv_copies[h]:
            c.wait()
        for first in range(h * half, (h + 1) * half, 4):
            group = range(first, first + 4)
            weights = []
            for r in group:
                score = lax.dot_general(
                    q[r], kc[r], (((1,), (1,)), ((), ())), preferred_element_type=f32
                )
                score = jnp.where(positions < lengths[r], score * inverse_root, -1e30)
                exponent = jnp.exp(score - jnp.max(score, axis=1, keepdims=True))
                total = jnp.sum(exponent, axis=1, keepdims=True)
                weights.append((exponent * (1.0 / total)).astype(bf16))
            for r, w in zip(group, weights):
                attn[r * heads_count : (r + 1) * heads_count] = jnp.dot(
                    w, vc[r], preferred_element_type=f32
                )
        for n in range(heads_count):
            gath[h * half : (h + 1) * half, n * head_dim : (n + 1) * head_dim] = attn[
                pl.ds(h * half * heads_count + n, half, stride=heads_count), :
            ].astype(bf16)
        if h == 0:
            pl.semaphore_wait(barrier, S)
        for direction in range(2):
            ring_copy(1, direction, h).start()
    for c in copies[1:]:
        c.start()

    bands = [jnp.zeros((1, rows), jnp.int32) for _ in range(top_count)]
    for k in range(top_count):
        named = chosen[k : k + 1, :]
        for e in range(experts):
            bands[k] = jnp.where(named == e, home[e], bands[k])
    band_ids = lax.broadcasted_iota(jnp.int32, (experts, rows), 0)
    member = jnp.zeros((experts, rows), f32)
    weight = jnp.zeros((experts, rows), f32)
    for k in range(top_count):
        member = jnp.where(band_ids == bands[k], 1.0, member)
        weight = jnp.where(band_ids == bands[k], probs[k : k + 1, :], weight)
    before = (
        lax.broadcasted_iota(jnp.int32, (rows, rows), 0)
        < lax.broadcasted_iota(jnp.int32, (rows, rows), 1)
    ).astype(bf16)
    rank = jnp.dot(member.astype(bf16), before, preferred_element_type=f32)
    rank = jnp.where(member > 0.0, rank, -1.0)
    places = lax.broadcasted_iota(jnp.int32, (cap, rows), 0).astype(f32)
    mix_parts = []
    for d in range(S):
        b = d // band_size
        hit = rank[b : b + 1, :] == places
        selector[d * cap : (d + 1) * cap] = jnp.where(hit, 1.0, 0.0).astype(bf16)
        mix_parts.append(jnp.where(hit, weight[b : b + 1, :], 0.0))
    mixing[...] = jnp.concatenate(mix_parts, axis=0).T

    def exchange(o):
        return remote(
            part.at[o, 1 - t],
            tp_in.at[o],
            tpx_send.at[o],
            tpx_recv.at[o],
            tp=1 - t,
        )

    def rel_of(o):
        if o == 0:
            return 0
        k = (o + 1) // 2
        return -k if o % 2 == 1 else k

    def feature_copy(o):
        return remote(
            feat_out.at[o],
            feat_in.at[s],
            feat_send.at[o],
            feat_recv.at[s],
            sect=owner(rel_of(o)),
        )

    def feature_arrival(j):
        return remote(feat_out.at[0], feat_in.at[j], feat_send.at[0], feat_recv.at[j], sect=j)

    def finish(o):
        exchange(o).wait_recv()
        total = part[o, t] + tp_in[o]
        if o == 0:
            feat_in[s] = total.astype(bf16)
        else:
            feat_out[o] = total.astype(bf16)
            feature_copy(o).start()

    def project(first, count):
        product = lax.dot_general(
            gath[first * rows : (first + count) * rows],
            wo[...],
            (((1,), (1,)), ((), ())),
            preferred_element_type=f32,
        )
        for b in range(count):
            for h in range(2):
                part[first + b, h] = product[b * rows + h * half : b * rows + (h + 1) * half]
            exchange(first + b).start()

    copies[0].wait()
    project(0, 1)
    waiting = [0]
    for k in range(1, ring_half + 1):
        for direction, h in ring_pairs(k):
            ring_copy(k, direction, h).wait_recv()
            if k < ring_half and (direction, h) in ring_pairs(k + 1):
                ring_copy(k + 1, direction, h).start()
        if k < ring_half:
            project(2 * k - 1, 2)
            for o in waiting:
                finish(o)
            waiting = [2 * k - 1, 2 * k]
        else:
            project(S - 1, 1)
            for o in waiting:
                finish(o)
            finish(S - 1)

    my_half = pl.ds(pl.multiple_of(t * half, half), half)
    their_half = pl.ds(pl.multiple_of((1 - t) * half, half), half)

    def await_features(d):
        feature_arrival((s + d) % S).wait_recv()

    each(S, 1, await_features)
    features = jnp.concatenate([feat_in[j].astype(f32) for j in range(S)], axis=1)
    a = resid[my_half, :].astype(f32) + features
    attended[my_half, :] = a
    scale = lax.rsqrt(jnp.sum(a * a, axis=1, keepdims=True) * (1.0 / D) + 1e-06)
    normed[my_half, :] = (a * scale * gain[...]).astype(bf16)
    normed_copy = remote(
        normed.at[my_half], normed.at[my_half], nx_send.at[0], nx_recv.at[0], tp=1 - t
    )
    normed_copy.start()

    def columns(core, c):
        return pl.ds(pl.multiple_of(core * H + starts[c], 128), widths[c])

    my_columns = pl.ds(pl.multiple_of(t * H, 128), H)
    their_columns = pl.ds(pl.multiple_of((1 - t) * H, 128), H)
    att_copy = remote(
        attended.at[my_half, their_columns],
        attended.at[my_half, their_columns],
        nx_send.at[1],
        nx_recv.at[1],
        tp=1 - t,
    )
    att_copy.start()
    remote(
        normed.at[their_half], normed.at[their_half], nx_send.at[0], nx_recv.at[0], tp=1 - t
    ).wait_recv()

    def slots_of(j):
        return pl.ds(pl.multiple_of(j * cap, cap), cap)

    def dispatch_copy(c, d):
        dest = (s + d) % S
        return remote(
            packed.at[slots_of(dest), pl.ds(starts[c], widths[c])],
            xbuf.at[slots_of(s), columns(t, c)],
            disp_send.at[c, d],
            disp_recv.at[c, d],
            sect=dest,
        )

    def dispatch_arrival(c, d):
        sender = (s - d + S) % S
        return remote(
            packed.at[slots_of(sender), pl.ds(starts[c], widths[c])],
            xbuf.at[slots_of(sender), columns(t, c)],
            disp_send.at[c, d],
            disp_recv.at[c, d],
            sect=sender,
        )

    def share_copy(c, core):
        block = xbuf.at[:, columns(core, c)]
        return remote(block, block, share_send.at[c], share_recv.at[c], tp=1 - t)

    for c in range(NC):
        packed[:, starts[c] : starts[c] + widths[c]] = jnp.dot(
            selector[...], normed[:, columns(t, c)], preferred_element_type=f32
        ).astype(bf16)
        each(S, 1, lambda d: dispatch_copy(c, d).start())
        xbuf[slots_of(s), columns(t, c)] = packed[
            slots_of(s), starts[c] : starts[c] + widths[c]
        ]

    copies[1].wait()
    copies[2].wait()

    def accumulate(c, core, first=False):
        x = xbuf[:, columns(core, c)]
        for m in range(2):
            product = jnp.dot(x, wg[m, columns(core, c), :], preferred_element_type=f32)
            if first:
                acc[m] = product
            else:
                acc[m] += product

    for c in range(NC):
        each(S, 1, lambda d: dispatch_arrival(c, d).wait_recv())
        share_copy(c, t).start()
        accumulate(c, t, first=c == 0)
        if c > 0:
            share_copy(c - 1, 1 - t).wait_recv()
            accumulate(c - 1, 1 - t)
    share_copy(NC - 1, 1 - t).wait_recv()
    accumulate(NC - 1, 1 - t)

    gate_value = acc[0]
    act[...] = (gate_value / (1.0 + jnp.exp(-gate_value)) * acc[1]).astype(bf16)
    copies[3].wait()

    def chunk(c):
        return pl.ds(starts[c], widths[c])

    def down_copy(c):
        return remote(
            down_out.at[:, chunk(c)],
            down_in.at[:, chunk(c)],
            dx_send.at[c],
            dx_recv.at[c],
            tp=1 - t,
        )

    def return_copy(c, d):
        dest = (s + d) % S
        return remote(
            ret_out.at[slots_of(dest), chunk(c)],
            ret_in.at[slots_of(s), chunk(c)],
            ret_send.at[c, d],
            ret_recv.at[c, d],
            sect=dest,
        )

    def return_arrival(c, d):
        sender = (s - d + S) % S
        return remote(
            ret_out.at[slots_of(sender), chunk(c)],
            ret_in.at[slots_of(sender), chunk(c)],
            ret_send.at[c, d],
            ret_recv.at[c, d],
            sect=sender,
        )

    for c in range(NC):
        cols = slice(starts[c], starts[c] + widths[c])
        down_out[:, cols] = jnp.dot(
            act[...], wd[:, columns(1 - t, c)], preferred_element_type=f32
        ).astype(bf16)
        down_copy(c).start()
        own = jnp.dot(act[...], wd[:, columns(t, c)], preferred_element_type=f32)
        down_copy(c).wait_recv()
        ret_out[:, cols] = (own.astype(bf16).astype(f32) + down_in[:, cols].astype(f32)).astype(
            bf16
        )
        each(S, 1, lambda d: return_copy(c, d).start())
        ret_in[slots_of(s), cols] = ret_out[slots_of(s), cols]

    mix = mixing[...]
    mix_high = mix.astype(bf16)
    rest = mix - mix_high.astype(f32)
    mix_mid = rest.astype(bf16)
    mix_low = (rest - mix_mid.astype(f32)).astype(bf16)
    remote(
        attended.at[their_half, my_columns],
        attended.at[their_half, my_columns],
        nx_send.at[1],
        nx_recv.at[1],
        tp=1 - t,
    ).wait_recv()
    for c in range(NC):
        cols = slice(starts[c], starts[c] + widths[c])
        each(S, 1, lambda d: return_arrival(c, d).wait_recv())
        got = ret_in[:, cols]
        expert_sum = (
            jnp.dot(mix_high, got, preferred_element_type=f32)
            + jnp.dot(mix_mid, got, preferred_element_type=f32)
            + jnp.dot(mix_low, got, preferred_element_type=f32)
        )
        out[:, cols] = (attended[:, columns(t, c)] + expert_sum).astype(bf16)

    for k in range(1, ring_half + 1):
        for direction, h in ring_pairs(k):
            ring_copy(k, direction, h).wait_send()
    for o in range(S):
        exchange(o).wait_send()
        if o > 0:
            feature_copy(o).wait_send()
    normed_copy.wait_send()
    att_copy.wait_send()
    for c in range(NC):
        each(S, 1, lambda d: dispatch_copy(c, d).wait_send())
        share_copy(c, t).wait_send()
        down_copy(c).wait_send()
        each(S, 1, lambda d: return_copy(c, d).wait_send())


def chunk_widths(total):
    unit = 256 if total % 256 == 0 else 128
    units = total // unit
    base, extra = units // 3, units % 3
    return tuple(unit * (base + (1 if c < extra else 0)) for c in range(3))


def layer_call(S, lengths, home, q, k, v, wo_t, resid, gain, chosen, probs, gate_up, down_proj):
    f32, bf16 = jnp.float32, jnp.bfloat16
    rows, heads_count, head_dim = q.shape
    half = rows // 2
    F = wo_t.shape[0]
    D = F * S
    hidden = down_proj.shape[0]
    slots = S * (rows // CAP_SHARE)
    widths = chunk_widths(D // 2)
    NC = len(widths)
    dma = pltpu.SemaphoreType.DMA
    vmem = pl.BlockSpec(memory_space=pltpu.VMEM)
    smem = pl.BlockSpec(memory_space=pltpu.SMEM)
    hbm = pl.BlockSpec(memory_space=pl.ANY)
    return pl.pallas_call(
        functools.partial(layer_kernel, S, widths),
        out_shape=jax.ShapeDtypeStruct((rows, D // 2), bf16),
        in_specs=[smem, smem, hbm, hbm, hbm, hbm, vmem, vmem, vmem, vmem, hbm, hbm],
        out_specs=vmem,
        scratch_shapes=[
            pltpu.VMEM(q.shape, bf16),
            pltpu.VMEM(k.shape, bf16),
            pltpu.VMEM(v.shape, bf16),
            pltpu.VMEM(wo_t.shape, bf16),
            pltpu.VMEM(gate_up.shape, bf16),
            pltpu.VMEM(down_proj.shape, bf16),
            pltpu.VMEM((rows * heads_count, head_dim), f32),
            pltpu.VMEM((S * rows, heads_count * head_dim), bf16),
            pltpu.VMEM((S, 2, half, F), f32),
            pltpu.VMEM((S, half, F), f32),
            pltpu.VMEM((S, half, F), bf16),
            pltpu.VMEM((S, half, F), bf16),
            pltpu.VMEM((rows, D), bf16),
            pltpu.VMEM((rows, D), f32),
            pltpu.VMEM((slots, rows), bf16),
            pltpu.VMEM((rows, slots), f32),
            pltpu.VMEM((slots, D // 2), bf16),
            pltpu.VMEM((slots, D), bf16),
            pltpu.VMEM((2, slots, hidden), f32),
            pltpu.VMEM((slots, hidden), bf16),
            pltpu.VMEM((slots, D // 2), bf16),
            pltpu.VMEM((slots, D // 2), bf16),
            pltpu.VMEM((slots, D // 2), bf16),
            pltpu.VMEM((slots, D // 2), bf16),
            dma((3, 2)),
            dma((4,)),
            dma((2, S // 2, 2)),
            dma((2, S // 2, 2)),
            dma((S,)),
            dma((S,)),
            dma((S,)),
            dma((S,)),
            dma((2,)),
            dma((2,)),
            dma((NC, S)),
            dma((NC, S)),
            dma((NC,)),
            dma((NC,)),
            dma((NC,)),
            dma((NC,)),
            dma((NC, S)),
            dma((NC, S)),
        ],
        compiler_params=pltpu.CompilerParams(
            collective_id=0, has_side_effects=True, vmem_limit_bytes=58 * 1024 * 1024
        ),
        cost_estimate=pl.CostEstimate(
            flops=2 * S * rows * wo_t.size + 6 * slots * D * hidden,
            bytes_accessed=2 * (wo_t.size + gate_up.size + down_proj.size),
            transcendentals=slots * hidden,
        ),
    )(lengths, home, q, k, v, wo_t, resid, gain, chosen, probs, gate_up, down_proj)


def body(
    queries,
    keys,
    values,
    kv_lengths,
    out_proj,
    resid,
    norm_gain,
    experts_chosen,
    route_probs,
    expert_home,
    gate_up,
    down_proj,
):
    row_count, context, _, head_dim = keys.shape
    return layer_call(
        lax.axis_size("sect"),
        kv_lengths,
        expert_home,
        queries,
        keys.reshape(row_count, context, head_dim),
        values.reshape(row_count, context, head_dim),
        out_proj.T,
        resid,
        norm_gain.astype(jnp.float32).reshape(1, -1),
        experts_chosen.T,
        route_probs.T,
        gate_up,
        down_proj,
    )


def solution(mesh):
    in_specs = (
        P(("groups", "sect"), "tp", None),
        P(("groups", "sect"), None, "tp", None),
        P(("groups", "sect"), None, "tp", None),
        P(("groups", "sect")),
        P("tp", "sect"),
        P(("groups", "sect"), None),
        P(),
        P(("groups", "sect"), None),
        P(("groups", "sect"), None),
        P(),
        P(None, None, ("sect", "tp")),
        P(("sect", "tp"), None),
    )
    out_specs = P(("groups", "sect"), "tp")
    return jax.shard_map(body, mesh=mesh, in_specs=in_specs, out_specs=out_specs, check_vma=False)
```

time: 92.3 us -> 70.1 us (0.76)
  local copies, waits for them, and re-layouts: 13.8 us -> 2.86 us
  other arithmetic: 5.33 us -> 0 us
  matrix products: 4.65 us -> 0 us
    unnamed x5 -> x1, local copies, waits for them, and re-layouts: 7.97 us -> 1.55 us
    dot_general x2 -> x0, matrix products: 4.65 us -> none  [the longest x1 3.05 us: body(): jnp.einsum('rkgc,rckd->rkgd', weights, values, preferred_element_type=jnp...]
    reshape x4 -> x1, local copies, waits for them, and re-layouts: 3.68 us -> 1.3 us  [body(): norm_gain.astype(jnp.float32).reshape(1, -1)]
    reduce_sum x2 -> x0, other arithmetic: 2.21 us -> none  [the longest x1 1.38 us: body(): mixing = jnp.sum(jnp.where(hits, route_probs[:, :, None], 0.0), axis=1)]
    convert_element_type x3 -> x0, other arithmetic: 1.7 us -> none  [the longest x1 1.61 us: body(): return (att + expert_sum).astype(jnp.bfloat16)]
    transpose x1 -> x0, local copies, waits for them, and re-layouts: 1.12 us -> none  [body(): att = att.transpose(0, 2, 1, 3).reshape(row_count, width // 2)]
where the time goes in v2:
time: 70.1 us; the launch traced here: 69.9 us
  Pallas kernels  67.1 us (96%)
  local copies, waits for them, and re-layouts  2.86 us (4%)
    pallas_call x1, Pallas kernels, layer_call(): pl.pallas_call(functools.partial(layer_kernel, S, widths), out_shape=jax....  67.1 us
    unnamed x1, local copies, waits for them, and re-layouts  1.55 us

profile of v2, /device:TPU:0, one launch (start us, length us, event | category | flops | bytes accessed | tf_op | source)
XLA Modules:
  0.0 69.9 jit_solution(6044583339356028926)
XLA Ops:
  0.0 1.3 %reshape.16.gain = f32[1,3584]{1,0:T(1,128)} reshape(bf16[3584]{0:T(1024)(128)(2,1)} %param.18) | data formatting | bytes 21504 | tf_op jit(solution)/shard_map/reshape | solution.py:584
  1.3 67.1 %shard_map.118 = bf16[32,1792]{1,0:T(8,128)(2,1)} custom-call(s32[32]{0:T(128)} %lengths.1, s32[8]{0:T(128)} %home.1, bf16[32,32,128]{2,1,0:T(8,128)(2,1)} %q_hbm.1, bf16[32,128,128]{2,1,0:T(8,128)(2,1)} %bitcast.6, bf16[32,128,128]{2,1,0:T(8,128)(2,1)} %bitcast.7, bf16[448,4096]{1,0:T(8,128)(2,1)} %bitcast.5, bf16[32,3584]{1,0:T(8,128)(2,1)} %resid.1, ...), custom_call_target="tpu_custom_call" | custom-call | flops 4462739456 | bytes 31195136 | tf_op jit(solution)/shard_map/pallas_call | solution.py:500
  68.4 1.6 %copy.14 = bf16[32,1792]{1,0:T(8,128)(2,1)} copy(bf16[32,1792]{1,0:T(8,128)(2,1)} %shard_map.118) | data formatting | bytes 229376

commit v3 on v2

--- a/solution.py
+++ b/solution.py
@@ -13,7 +13,7 @@
 
 def each(count, start, f):
     if count <= 8:
-        for i in range(start, count):
+        for i in sorted(range(start, count), key=lambda i: -min(i, count - i)):
             f(i)
     else:
 
@@ -98,7 +98,9 @@
     top_count = chosen.shape[0]
     NC = len(widths)
     starts = [sum(widths[:c]) for c in range(NC)]
+    back, back_starts = widths[::-1], starts[::-1]
     ring_half = S // 2
+    K_half = heads_count * head_dim // 2
 
     def ring_index(p):
         return jnp.where(p < ring_half, 2 * p, 2 * (S - 1 - p) + 1)
@@ -160,6 +162,15 @@
         return 2 * k - 1 if direction == 0 or k == ring_half else 2 * k
 
     def ring_copy(k, direction, h):
+        if k == ring_half:
+            cols = pl.ds(h * K_half, K_half)
+            return remote(
+                gath.at[pl.ds(slot(k - 1, direction) * rows + direction * half, half), cols],
+                gath.at[pl.ds(slot(k, direction) * rows + direction * half, half), cols],
+                ring_send.at[direction, k - 1, h],
+                ring_recv.at[direction, k - 1, h],
+                sect=right if direction == 0 else left,
+            )
         return remote(
             gath.at[pl.ds(slot(k - 1, direction) * rows + h * half, half)],
             gath.at[pl.ds(slot(k, direction) * rows + h * half, half)],
@@ -168,8 +179,7 @@
             sect=right if direction == 0 else left,
         )
 
-    def ring_pairs(k):
-        return [(0, 0), (1, 1)] if k == ring_half else [(0, 0), (1, 0), (0, 1), (1, 1)]
+    ring_pairs = [(0, 0), (1, 0), (0, 1), (1, 1)]
 
     positions = lax.broadcasted_iota(jnp.int32, (heads_count, context), 1)
     inverse_root = 1.0 / math.sqrt(head_dim)
@@ -264,36 +274,46 @@
             feat_out[o] = total.astype(bf16)
             feature_copy(o).start()
 
-    def project(first, count):
-        product = lax.dot_general(
-            gath[first * rows : (first + count) * rows],
-            wo[...],
+    def product_of(first, count, cols):
+        return lax.dot_general(
+            gath[first * rows : (first + count) * rows, cols],
+            wo[:, cols],
             (((1,), (1,)), ((), ())),
             preferred_element_type=f32,
         )
+
+    def project(first, count, product):
         for b in range(count):
             for h in range(2):
                 part[first + b, h] = product[b * rows + h * half : b * rows + (h + 1) * half]
             exchange(first + b).start()
 
     copies[0].wait()
-    project(0, 1)
+    project(0, 1, product_of(0, 1, slice(None)))
     waiting = [0]
-    for k in range(1, ring_half + 1):
-        for direction, h in ring_pairs(k):
+    for k in range(1, ring_half):
+        for direction, h in ring_pairs:
             ring_copy(k, direction, h).wait_recv()
-            if k < ring_half and (direction, h) in ring_pairs(k + 1):
+            if k + 1 < ring_half:
                 ring_copy(k + 1, direction, h).start()
-        if k < ring_half:
-            project(2 * k - 1, 2)
-            for o in waiting:
-                finish(o)
-            waiting = [2 * k - 1, 2 * k]
-        else:
-            project(S - 1, 1)
-            for o in waiting:
-                finish(o)
-            finish(S - 1)
+            elif direction == h:
+                ring_copy(k + 1, direction, 0).start()
+                ring_copy(k + 1, direction, 1).start()
+            if (direction, h) == (1, 0):
+                for o in waiting:
+                    finish(o)
+        project(2 * k - 1, 2, product_of(2 * k - 1, 2, slice(None)))
+        waiting = [2 * k - 1, 2 * k]
+    for o in waiting:
+        finish(o)
+    product = None
+    for h in range(2):
+        for direction in range(2):
+            ring_copy(ring_half, direction, h).wait_recv()
+        more = product_of(S - 1, 1, slice(h * K_half, (h + 1) * K_half))
+        product = more if product is None else product + more
+    project(S - 1, 1, product)
+    finish(S - 1)
 
     my_half = pl.ds(pl.multiple_of(t * half, half), half)
     their_half = pl.ds(pl.multiple_of((1 - t) * half, half), half)
@@ -306,7 +326,7 @@
     a = resid[my_half, :].astype(f32) + features
     attended[my_half, :] = a
     scale = lax.rsqrt(jnp.sum(a * a, axis=1, keepdims=True) * (1.0 / D) + 1e-06)
-    normed[my_half, :] = (a * scale * gain[...]).astype(bf16)
+    normed[my_half, :] = (a * scale * gain[...].astype(f32).reshape(1, D)).astype(bf16)
     normed_copy = remote(
         normed.at[my_half], normed.at[my_half], nx_send.at[0], nx_recv.at[0], tp=1 - t
     )
@@ -392,7 +412,7 @@
     copies[3].wait()
 
     def chunk(c):
-        return pl.ds(starts[c], widths[c])
+        return pl.ds(back_starts[c], back[c])
 
     def down_copy(c):
         return remote(
@@ -424,12 +444,12 @@
         )
 
     for c in range(NC):
-        cols = slice(starts[c], starts[c] + widths[c])
+        cols = slice(back_starts[c], back_starts[c] + back[c])
         down_out[:, cols] = jnp.dot(
-            act[...], wd[:, columns(1 - t, c)], preferred_element_type=f32
+            act[...], wd[:, columns(1 - t, NC - 1 - c)], preferred_element_type=f32
         ).astype(bf16)
         down_copy(c).start()
-        own = jnp.dot(act[...], wd[:, columns(t, c)], preferred_element_type=f32)
+        own = jnp.dot(act[...], wd[:, columns(t, NC - 1 - c)], preferred_element_type=f32)
         down_copy(c).wait_recv()
         ret_out[:, cols] = (own.astype(bf16).astype(f32) + down_in[:, cols].astype(f32)).astype(
             bf16
@@ -450,7 +470,7 @@
         tp=1 - t,
     ).wait_recv()
     for c in range(NC):
-        cols = slice(starts[c], starts[c] + widths[c])
+        cols = slice(back_starts[c], back_starts[c] + back[c])
         each(S, 1, lambda d: return_arrival(c, d).wait_recv())
         got = ret_in[:, cols]
         expert_sum = (
@@ -458,10 +478,10 @@
             + jnp.dot(mix_mid, got, preferred_element_type=f32)
             + jnp.dot(mix_low, got, preferred_element_type=f32)
         )
-        out[:, cols] = (attended[:, columns(t, c)] + expert_sum).astype(bf16)
+        out[:, cols] = (attended[:, columns(t, NC - 1 - c)] + expert_sum).astype(bf16)
 
     for k in range(1, ring_half + 1):
-        for direction, h in ring_pairs(k):
+        for direction, h in ring_pairs:
             ring_copy(k, direction, h).wait_send()
     for o in range(S):
         exchange(o).wait_send()
@@ -479,8 +499,8 @@
 def chunk_widths(total):
     unit = 256 if total % 256 == 0 else 128
     units = total // unit
-    base, extra = units // 3, units % 3
-    return tuple(unit * (base + (1 if c < extra else 0)) for c in range(3))
+    widths = [2 * unit] * (units // 2)
+    return tuple(widths + [unit] * (units % 2))
 
 
 def layer_call(S, lengths, home, q, k, v, wo_t, resid, gain, chosen, probs, gate_up, down_proj):
@@ -499,7 +519,7 @@
     hbm = pl.BlockSpec(memory_space=pl.ANY)
     return pl.pallas_call(
         functools.partial(layer_kernel, S, widths),
-        out_shape=jax.ShapeDtypeStruct((rows, D // 2), bf16),
+        out_shape=pltpu.VMEM((rows, D // 2), bf16),
         in_specs=[smem, smem, hbm, hbm, hbm, hbm, vmem, vmem, vmem, vmem, hbm, hbm],
         out_specs=vmem,
         scratch_shapes=[
@@ -547,7 +567,7 @@
             dma((NC, S)),
         ],
         compiler_params=pltpu.CompilerParams(
-            collective_id=0, has_side_effects=True, vmem_limit_bytes=58 * 1024 * 1024
+            collective_id=0, has_side_effects=True, vmem_limit_bytes=60 * 1024 * 1024
         ),
         cost_estimate=pl.CostEstimate(
             flops=2 * S * rows * wo_t.size + 6 * slots * D * hidden,
@@ -581,7 +601,7 @@
         values.reshape(row_count, context, head_dim),
         out_proj.T,
         resid,
-        norm_gain.astype(jnp.float32).reshape(1, -1),
+        norm_gain,
         experts_chosen.T,
         route_probs.T,
         gate_up,

time: 70.1 us -> 67.6 us (0.964)
  local copies, waits for them, and re-layouts: 2.86 us -> 0.65 us
    reshape x1 -> x0, local copies, waits for them, and re-layouts: 1.3 us -> none  [body(): norm_gain.astype(jnp.float32).reshape(1, -1)]
    unnamed x1, local copies, waits for them, and re-layouts: 1.55 us -> 0.65 us
where the time goes in v3:
time: 67.6 us; the launch traced here: 67.5 us
  Pallas kernels  66.8 us (99%)
    pallas_call x1, Pallas kernels, layer_call(): pl.pallas_call(functools.partial(layer_kernel, S, widths), out_shape=pltp...  66.8 us

profile of v3, /device:TPU:0, one launch (start us, length us, event | category | flops | bytes accessed | tf_op | source)
XLA Modules:
  0.0 67.5 jit_solution(8490235294267370460)
XLA Ops:
  0.0 66.8 %shard_map.118 = bf16[32,1792]{1,0:T(8,128)(2,1)S(1)} custom-call(s32[32]{0:T(128)} %lengths.1, s32[8]{0:T(128)} %home.1, bf16[32,32,128]{2,1,0:T(8,128)(2,1)} %q_hbm.1, bf16[32,128,128]{2,1,0:T(8,128)(2,1)} %bitcast.6, bf16[32,128,128]{2,1,0:T(8,128)(2,1)} %bitcast.7, bf16[448,4096]{1,0:T(8,128)(2,1)} %bitcast.5, bf16[32,3584]{1,0:T(8,128)(2,1)} %resid.1, ...), custom_call_target="tpu_custom_call" | custom-call | flops 4462739456 | bytes 31195136 | tf_op jit(solution)/shard_map/pallas_call | solution.py:520
  66.8 0.6 copy.14

commit v4 on v3

--- a/solution.py
+++ b/solution.py
@@ -22,6 +22,19 @@
             return carry
 
         lax.fori_loop(start, count, step, 0)
+
+
+def each_partner(S, batch, f):
+    if S <= 8:
+        for d in sorted(range(2 - batch, S, 2), key=lambda d: -min(d, S - d)):
+            f(d)
+    else:
+
+        def step(i, carry):
+            f(2 * i + batch)
+            return carry
+
+        lax.fori_loop(1 - batch, S // 2, step, 0)
 
 
 def layer_kernel(
@@ -92,7 +105,7 @@
     F = wo.shape[0]
     D = F * S
     H = D // 2
-    cap = xbuf.shape[0] // S
+    cap = packed.shape[0] // S
     experts = home.shape[0]
     band_size = S // experts
     top_count = chosen.shape[0]
@@ -236,7 +249,8 @@
         hit = rank[b : b + 1, :] == places
         selector[d * cap : (d + 1) * cap] = jnp.where(hit, 1.0, 0.0).astype(bf16)
         mix_parts.append(jnp.where(hit, weight[b : b + 1, :], 0.0))
-    mixing[...] = jnp.concatenate(mix_parts, axis=0).T
+    for parity in range(2):
+        mixing[parity] = jnp.concatenate(mix_parts[parity::2], axis=0).T
 
     def exchange(o):
         return remote(
@@ -352,44 +366,49 @@
     def slots_of(j):
         return pl.ds(pl.multiple_of(j * cap, cap), cap)
 
-    def dispatch_copy(c, d):
+    def pair_slots(j):
+        return slots_of(j // 2)
+
+    def dispatch_copy(c, d, batch):
         dest = (s + d) % S
         return remote(
             packed.at[slots_of(dest), pl.ds(starts[c], widths[c])],
-            xbuf.at[slots_of(s), columns(t, c)],
+            xbuf.at[batch, pair_slots(s), columns(t, c)],
             disp_send.at[c, d],
             disp_recv.at[c, d],
             sect=dest,
         )
 
-    def dispatch_arrival(c, d):
+    def dispatch_arrival(c, d, batch):
         sender = (s - d + S) % S
         return remote(
             packed.at[slots_of(sender), pl.ds(starts[c], widths[c])],
-            xbuf.at[slots_of(sender), columns(t, c)],
+            xbuf.at[batch, pair_slots(sender), columns(t, c)],
             disp_send.at[c, d],
             disp_recv.at[c, d],
             sect=sender,
         )
 
-    def share_copy(c, core):
-        block = xbuf.at[:, columns(core, c)]
-        return remote(block, block, share_send.at[c], share_recv.at[c], tp=1 - t)
+    def share_copy(c, core, batch):
+        block = xbuf.at[batch, :, columns(core, c)]
+        return remote(block, block, share_send.at[batch, c], share_recv.at[batch, c], tp=1 - t)
 
     for c in range(NC):
         packed[:, starts[c] : starts[c] + widths[c]] = jnp.dot(
             selector[...], normed[:, columns(t, c)], preferred_element_type=f32
         ).astype(bf16)
-        each(S, 1, lambda d: dispatch_copy(c, d).start())
-        xbuf[slots_of(s), columns(t, c)] = packed[
+        each_partner(S, 0, lambda d: dispatch_copy(c, d, 0).start())
+        xbuf[0, pair_slots(s), columns(t, c)] = packed[
             slots_of(s), starts[c] : starts[c] + widths[c]
         ]
+    for c in range(NC):
+        each_partner(S, 1, lambda d: dispatch_copy(c, d, 1).start())
 
     copies[1].wait()
     copies[2].wait()
 
-    def accumulate(c, core, first=False):
-        x = xbuf[:, columns(core, c)]
+    def accumulate(c, core, batch, first=False):
+        x = xbuf[batch, :, columns(core, c)]
         for m in range(2):
             product = jnp.dot(x, wg[m, columns(core, c), :], preferred_element_type=f32)
             if first:
@@ -397,71 +416,72 @@
             else:
                 acc[m] += product
 
-    for c in range(NC):
-        each(S, 1, lambda d: dispatch_arrival(c, d).wait_recv())
-        share_copy(c, t).start()
-        accumulate(c, t, first=c == 0)
-        if c > 0:
-            share_copy(c - 1, 1 - t).wait_recv()
-            accumulate(c - 1, 1 - t)
-    share_copy(NC - 1, 1 - t).wait_recv()
-    accumulate(NC - 1, 1 - t)
-
-    gate_value = acc[0]
-    act[...] = (gate_value / (1.0 + jnp.exp(-gate_value)) * acc[1]).astype(bf16)
-    copies[3].wait()
-
     def chunk(c):
         return pl.ds(back_starts[c], back[c])
 
-    def down_copy(c):
-        return remote(
-            down_out.at[:, chunk(c)],
-            down_in.at[:, chunk(c)],
-            dx_send.at[c],
-            dx_recv.at[c],
+    def down_copy(c, batch):
+        return remote(
+            down_out.at[batch, :, chunk(c)],
+            down_in.at[batch, :, chunk(c)],
+            dx_send.at[batch, c],
+            dx_recv.at[batch, c],
             tp=1 - t,
         )
 
-    def return_copy(c, d):
+    def return_copy(c, d, batch):
         dest = (s + d) % S
         return remote(
-            ret_out.at[slots_of(dest), chunk(c)],
-            ret_in.at[slots_of(s), chunk(c)],
+            ret_out.at[batch, pair_slots(dest), chunk(c)],
+            ret_in.at[batch, pair_slots(s), chunk(c)],
             ret_send.at[c, d],
             ret_recv.at[c, d],
             sect=dest,
         )
 
-    def return_arrival(c, d):
+    def return_arrival(c, d, batch):
         sender = (s - d + S) % S
         return remote(
-            ret_out.at[slots_of(sender), chunk(c)],
-            ret_in.at[slots_of(sender), chunk(c)],
+            ret_out.at[batch, pair_slots(sender), chunk(c)],
+            ret_in.at[batch, pair_slots(sender), chunk(c)],
             ret_send.at[c, d],
             ret_recv.at[c, d],
             sect=sender,
         )
 
-    for c in range(NC):
-        cols = slice(back_starts[c], back_starts[c] + back[c])
-        down_out[:, cols] = jnp.dot(
-            act[...], wd[:, columns(1 - t, NC - 1 - c)], preferred_element_type=f32
-        ).astype(bf16)
-        down_copy(c).start()
-        own = jnp.dot(act[...], wd[:, columns(t, NC - 1 - c)], preferred_element_type=f32)
-        down_copy(c).wait_recv()
-        ret_out[:, cols] = (own.astype(bf16).astype(f32) + down_in[:, cols].astype(f32)).astype(
-            bf16
-        )
-        each(S, 1, lambda d: return_copy(c, d).start())
-        ret_in[slots_of(s), cols] = ret_out[slots_of(s), cols]
-
-    mix = mixing[...]
-    mix_high = mix.astype(bf16)
-    rest = mix - mix_high.astype(f32)
-    mix_mid = rest.astype(bf16)
-    mix_low = (rest - mix_mid.astype(f32)).astype(bf16)
+    for batch in range(2):
+        for c in range(NC):
+            each_partner(S, batch, lambda d: dispatch_arrival(c, d, batch).wait_recv())
+            share_copy(c, t, batch).start()
+            accumulate(c, t, batch, first=c == 0)
+            if c > 0:
+                share_copy(c - 1, 1 - t, batch).wait_recv()
+                accumulate(c - 1, 1 - t, batch)
+        share_copy(NC - 1, 1 - t, batch).wait_recv()
+        accumulate(NC - 1, 1 - t, batch)
+
+        gate_value = acc[0]
+        act[...] = (gate_value / (1.0 + jnp.exp(-gate_value)) * acc[1]).astype(bf16)
+        if batch == 0:
+            copies[3].wait()
+        for c in range(NC):
+            cols = slice(back_starts[c], back_starts[c] + back[c])
+            down_out[batch, :, cols] = jnp.dot(
+                act[...], wd[:, columns(1 - t, NC - 1 - c)], preferred_element_type=f32
+            ).astype(bf16)
+            down_copy(c, batch).start()
+        for c in range(NC):
+            cols = slice(back_starts[c], back_starts[c] + back[c])
+            own = jnp.dot(
+                act[...], wd[:, columns(t, NC - 1 - c)], preferred_element_type=f32
+            ).astype(bf16)
+            down_copy(c, batch).wait_recv()
+            ret_out[batch, :, cols] = (
+                own.astype(f32) + down_in[batch, :, cols].astype(f32)
+            ).astype(bf16)
+            each_partner(S, batch, lambda d: return_copy(c, d, batch).start())
+            if batch == 0:
+                ret_in[0, pair_slots(s), cols] = ret_out[0, pair_slots(s), cols]
+
     remote(
         attended.at[their_half, my_columns],
         attended.at[their_half, my_columns],
@@ -469,16 +489,26 @@
         nx_recv.at[1],
         tp=1 - t,
     ).wait_recv()
-    for c in range(NC):
-        cols = slice(back_starts[c], back_starts[c] + back[c])
-        each(S, 1, lambda d: return_arrival(c, d).wait_recv())
-        got = ret_in[:, cols]
-        expert_sum = (
-            jnp.dot(mix_high, got, preferred_element_type=f32)
-            + jnp.dot(mix_mid, got, preferred_element_type=f32)
-            + jnp.dot(mix_low, got, preferred_element_type=f32)
-        )
-        out[:, cols] = (attended[:, columns(t, NC - 1 - c)] + expert_sum).astype(bf16)
+    for batch in range(2):
+        mix = mixing[(s + batch) % 2]
+        mix_high = mix.astype(bf16)
+        rest = mix - mix_high.astype(f32)
+        mix_mid = rest.astype(bf16)
+        mix_low = (rest - mix_mid.astype(f32)).astype(bf16)
+        for c in range(NC):
+            cols = slice(back_starts[c], back_starts[c] + back[c])
+            each_partner(S, batch, lambda d: return_arrival(c, d, batch).wait_recv())
+            got = ret_in[batch, :, cols]
+            expert_sum = (
+                jnp.dot(mix_high, got, preferred_element_type=f32)
+                + jnp.dot(mix_mid, got, preferred_element_type=f32)
+                + jnp.dot(mix_low, got, preferred_element_type=f32)
+            )
+            total = attended[:, columns(t, NC - 1 - c)] + expert_sum
+            if batch == 0:
+                attended[:, columns(t, NC - 1 - c)] = total
+            else:
+                out[:, cols] = total.astype(bf16)
 
     for k in range(1, ring_half + 1):
         for direction, h in ring_pairs:
@@ -490,10 +520,11 @@
     normed_copy.wait_send()
     att_copy.wait_send()
     for c in range(NC):
-        each(S, 1, lambda d: dispatch_copy(c, d).wait_send())
-        share_copy(c, t).wait_send()
-        down_copy(c).wait_send()
-        each(S, 1, lambda d: return_copy(c, d).wait_send())
+        for batch in range(2):
+            each_partner(S, batch, lambda d: dispatch_copy(c, d, batch).wait_send())
+            share_copy(c, t, batch).wait_send()
+            down_copy(c, batch).wait_send()
+            each_partner(S, batch, lambda d: return_copy(c, d, batch).wait_send())
 
 
 def chunk_widths(total):
@@ -538,15 +569,15 @@
             pltpu.VMEM((rows, D), bf16),
             pltpu.VMEM((rows, D), f32),
             pltpu.VMEM((slots, rows), bf16),
-            pltpu.VMEM((rows, slots), f32),
+            pltpu.VMEM((2, rows, slots // 2), f32),
             pltpu.VMEM((slots, D // 2), bf16),
-            pltpu.VMEM((slots, D), bf16),
-            pltpu.VMEM((2, slots, hidden), f32),
-            pltpu.VMEM((slots, hidden), bf16),
-            pltpu.VMEM((slots, D // 2), bf16),
-            pltpu.VMEM((slots, D // 2), bf16),
-            pltpu.VMEM((slots, D // 2), bf16),
-            pltpu.VMEM((slots, D // 2), bf16),
+            pltpu.VMEM((2, slots // 2, D), bf16),
+            pltpu.VMEM((2, slots // 2, hidden), f32),
+            pltpu.VMEM((slots // 2, hidden), bf16),
+            pltpu.VMEM((2, slots // 2, D // 2), bf16),
+            pltpu.VMEM((2, slots // 2, D // 2), bf16),
+            pltpu.VMEM((2, slots // 2, D // 2), bf16),
+            pltpu.VMEM((2, slots // 2, D // 2), bf16),
             dma((3, 2)),
             dma((4,)),
             dma((2, S // 2, 2)),
@@ -559,10 +590,10 @@
             dma((2,)),
             dma((NC, S)),
             dma((NC, S)),
-            dma((NC,)),
-            dma((NC,)),
-            dma((NC,)),
-            dma((NC,)),
+            dma((2, NC)),
+            dma((2, NC)),
+            dma((2, NC)),
+            dma((2, NC)),
             dma((NC, S)),
             dma((NC, S)),
         ],

time: 67.6 us -> 65 us (0.962)
  Pallas kernels: 66.8 us -> 64.2 us
    pallas_call x1, Pallas kernels: 66.8 us -> 64.2 us  [layer_call(): pl.pallas_call(functools.partial(layer_kernel, S, widths), out_shape=pltp...]
where the time goes in v4:
time: 65 us; the launch traced here: 64.8 us
  Pallas kernels  64.2 us (99%)
  local copies, waits for them, and re-layouts  0.65 us (1%)
    pallas_call x1, Pallas kernels, layer_call(): pl.pallas_call(functools.partial(layer_kernel, S, widths), out_shape=pltp...  64.2 us

profile of v4, /device:TPU:0, one launch (start us, length us, event | category | flops | bytes accessed | tf_op | source)
XLA Modules:
  0.0 64.8 jit_solution(12702992582201849122)
XLA Ops:
  0.0 64.2 %shard_map.118 = bf16[32,1792]{1,0:T(8,128)(2,1)S(1)} custom-call(s32[32]{0:T(128)} %lengths.1, s32[8]{0:T(128)} %home.1, bf16[32,32,128]{2,1,0:T(8,128)(2,1)} %q_hbm.1, bf16[32,128,128]{2,1,0:T(8,128)(2,1)} %bitcast.6, bf16[32,128,128]{2,1,0:T(8,128)(2,1)} %bitcast.7, bf16[448,4096]{1,0:T(8,128)(2,1)} %bitcast.5, bf16[32,3584]{1,0:T(8,128)(2,1)} %resid.1, ...), custom_call_target="tpu_custom_call" | custom-call | flops 4462739456 | bytes 31195136 | tf_op jit(solution)/shard_map/pallas_call | solution.py:551
  64.2 0.6 %copy.14 = bf16[32,1792]{1,0:T(8,128)(2,1)} copy(bf16[32,1792]{1,0:T(8,128)(2,1)S(1)} %shard_map.118) | data formatting | bytes 229376
